TPU v7x, 512 devices: a whole 4x8x8 slice. The times are simulated.
512 devices in a mesh: row: 16 (over z, core), col: 32 (over y, x).
Axes of the slice: x: 4, y: 8, z: 8, core: 2. Of those that a mesh axis runs over, the one named last changes fastest.
Arguments:
- grad_out: bfloat16 [1536, 16384], P('row', 'col'), may hold values from -1.59375 to 1.59375
- gate_pre: bfloat16 [1536, 13312], P('col', 'row'), may hold values from -10 to 10
- up_pre: bfloat16 [1536, 13312], P('col', 'row'), may hold values from -6 to 6
- down_weight: bfloat16 [13312, 16384], P('row', 'col'), may hold values from -0.046875 to 0.046875
- gate_weight: bfloat16 [16384, 13312], P('col', 'row'), may hold values from -0.09375 to 0.09375
- up_weight: bfloat16 [16384, 13312], P('col', 'row'), may hold values from -0.09375 to 0.09375
Outputs:
- input_grad: bfloat16 [1536, 16384], P('row', 'col')
- down_grad: bfloat16 [13312, 16384], P('row', 'col')
All inputs are finite; a program needn't handle non-finite values.
Results may differ from a plain program's by a relative error of at most 0.039.
Values may be sent and summed in bfloat16 or wider, within the bound.
A program may use at most 64 MiB of HBM per device.

v0:
```python
import jax
import jax.numpy as jnp
from jax import lax
from jax.sharding import PartitionSpec as P


def swiglu_back(hidden_grad, gate_pre, up_pre):
    gate_value = gate_pre.astype(jnp.float32)
    up_value = up_pre.astype(jnp.float32)
    sigmoid_gate = jax.nn.sigmoid(gate_value)
    activated = gate_value * sigmoid_gate
    hidden = (activated * up_value).astype(jnp.bfloat16)
    up_grad = (hidden_grad * activated).astype(jnp.bfloat16)
    gate_grad = (
        hidden_grad * up_value * sigmoid_gate * (1.0 + gate_value * (1.0 - sigmoid_gate))
    ).astype(jnp.bfloat16)
    return (hidden, gate_grad, up_grad)


def on_device(grad_out, gate_pre, up_pre, down_weight, gate_weight, up_weight):
    grad_rows = lax.all_gather(grad_out, "row", axis=0, tiled=True)
    hidden_grad = lax.psum_scatter(
        lax.dot_general(
            grad_rows, down_weight, (((1,), (1,)), ((), ())), preferred_element_type=jnp.float32
        ).astype(jnp.bfloat16),
        "col",
        scatter_dimension=0,
        tiled=True,
    ).astype(jnp.float32)
    hidden, gate_grad, up_grad = swiglu_back(hidden_grad, gate_pre, up_pre)
    hidden, gate_grad, up_grad = (
        lax.all_gather(hidden, "col", axis=0, tiled=True),
        lax.all_gather(gate_grad, "col", axis=0, tiled=True),
        lax.all_gather(up_grad, "col", axis=0, tiled=True),
    )
    down_grad = lax.dot_general(
        hidden, grad_rows, (((0,), (0,)), ((), ())), preferred_element_type=jnp.float32
    ).astype(jnp.bfloat16)
    summed = lax.dot_general(
        gate_grad, gate_weight, (((1,), (1,)), ((), ())), preferred_element_type=jnp.float32
    )
    input_grad = lax.psum_scatter(
        (
            summed
            + lax.dot_general(
                up_grad, up_weight, (((1,), (1,)), ((), ())), preferred_element_type=jnp.float32
            )
        ).astype(jnp.bfloat16),
        "row",
        scatter_dimension=0,
        tiled=True,
    )
    return (input_grad, down_grad)


def solution(mesh):
    placed = (
        P("row", "col"),
        P("col", "row"),
        P("col", "row"),
        P("row", "col"),
        P("col", "row"),
        P("col", "row"),
    )
    return jax.shard_map(
        on_device,
        mesh=mesh,
        in_specs=placed,
        out_specs=(P("row", "col"), P("row", "col")),
        check_vma=False,
    )
```

profile of v0, /device:TPU:18, one launch (start us, length us, event | category | flops | bytes accessed | tf_op | source)
XLA Modules:
  0.0 600.0 jit_solution(16523458400923756926)
XLA Ops:
  7.2 0.0 copy-start
  7.2 0.0 all-gather.5.cloned.1.call-start
  7.2 0.7 all-gather.5.cloned.1.call-update
  7.9 0.0 reduce-scatter.3.cloned.1.call-start
  8.0 49.2 %all-gather.5.cloned.1.call-done = bf16[1536,512]{1,0:T(8,128)(2,1)} async-done(((bf16[96,512]{1,0:T(8,128)(2,1)}), bf16[1536,512]{1,0:T(8,128)(2,1)}) %all-gather.5.cloned.1.call-update) | async-done | bytes 1572880 | tf_op jit(solution)/shard_map/all_gather | solution.py:21
  57.1 0.0 copy-done
  57.1 4.8 convolution_convert_fusion
  61.9 0.0 copy-start.1
  61.9 0.0 copy-start.2
  61.9 0.0 copy-start.4
  61.9 0.0 reduce-scatter.3.cloned.1.call-update
  62.0 0.0 all-gather.7.cloned.1.call-start
  62.0 208.6 %reduce-scatter.3.cloned.1.call-done = bf16[48,832]{1,0:T(8,128)(2,1)} async-done(((bf16[1536,832]{1,0:T(8,128)(2,1)}), bf16[48,832]{1,0:T(8,128)(2,1)}) %reduce-scatter.3.cloned.1.call-update) | async-done | bytes 79888 | tf_op jit(solution)/shard_map/reduce_scatter | solution.py:22
  270.6 0.0 copy-done.1
  270.6 0.0 copy-done.2
  270.6 1.7 fusion.5
  272.3 0.0 all-gather.7.cloned.1.call-update
  272.3 0.0 all-gather.9.cloned.1.call-start
  272.4 0.5 all-gather.9.cloned.1.call-update
  272.9 0.0 all-gather.11.cloned.1.call-start
  273.0 0.5 all-gather.11.cloned.1.call-update
  273.5 0.0 copy-start.5
  273.5 0.0 reduce-scatter.5.cloned.1.call-start
  273.6 83.8 %all-gather.7.cloned.1.call-done = bf16[1536,832]{1,0:T(8,128)(2,1)} async-done(((bf16[48,832]{1,0:T(8,128)(2,1)}), bf16[1536,832]{1,0:T(8,128)(2,1)}) %all-gather.7.cloned.1.call-update) | async-done | bytes 2555920 | tf_op jit(solution)/shard_map/all_gather | solution.py:33
  357.3 0.0 copy-done.4
  357.3 5.2 fusion.10
  362.6 0.0 copy-start.3
  362.6 80.0 %all-gather.9.cloned.1.call-done = bf16[1536,832]{1,0:T(8,128)(2,1)} async-done(((bf16[48,832]{1,0:T(8,128)(2,1)}), bf16[1536,832]{1,0:T(8,128)(2,1)}) %all-gather.9.cloned.1.call-update) | async-done | bytes 2555920 | tf_op jit(solution)/shard_map/all_gather | solution.py:34
  442.6 0.0 copy-done.5
  442.6 5.7 fusion
  448.3 0.0 reduce-scatter.5.cloned.1.call-update
  448.3 80.1 %all-gather.11.cloned.1.call-done = bf16[1536,832]{1,0:T(8,128)(2,1)} async-done(((bf16[48,832]{1,0:T(8,128)(2,1)}), bf16[1536,832]{1,0:T(8,128)(2,1)}) %all-gather.11.cloned.1.call-update) | async-done | bytes 2555920 | tf_op jit(solution)/shard_map/all_gather | solution.py:32
  528.5 0.0 copy-done.3
  528.5 4.2 convolution_convert_fusion.1
  532.6 60.5 %reduce-scatter.5.cloned.1.call-done = bf16[96,512]{1,0:T(8,128)(2,1)} async-done(((bf16[1536,512]{1,0:T(8,128)(2,1)}), bf16[96,512]{1,0:T(8,128)(2,1)}) %reduce-scatter.5.cloned.1.call-update) | async-done | bytes 98320 | tf_op jit(solution)/shard_map/reduce_scatter | solution.py:42
Async XLA Ops:
  7.2 50.0 %copy-start = (bf16[832,512]{1,0:T(8,128)(2,1)S(1)}, bf16[832,512]{1,0:T(8,128)(2,1)}, u32[]{:S(2)}) copy-start(bf16[832,512]{1,0:T(8,128)(2,1)} %param.9) | copy-start | bytes 2555908
  7.2 50.0 %all-gather.5.cloned.1.call-start = ((), (), s32[]{:S(2)}) async-start(), calls=%async_computation.2 | async-start | bytes 1671168 | tf_op jit(solution)/shard_map/all_gather | solution.py:21
  7.9 262.7 %reduce-scatter.3.cloned.1.call-start = ((), (), s32[]{:S(2)}) async-start(), calls=%async_computation.3 | async-start | bytes 2838528 | tf_op jit(solution)/shard_map/reduce_scatter | solution.py:22
  61.9 208.7 %copy-start.1 = (bf16[48,832]{1,0:T(8,128)(2,1)S(1)}, bf16[48,832]{1,0:T(8,128)(2,1)}, u32[]{:S(2)}) copy-start(bf16[48,832]{1,0:T(8,128)(2,1)} %param.8) | copy-start | bytes 239620
  61.9 208.7 %copy-start.2 = (bf16[48,832]{1,0:T(8,128)(2,1)S(1)}, bf16[48,832]{1,0:T(8,128)(2,1)}, u32[]{:S(2)}) copy-start(bf16[48,832]{1,0:T(8,128)(2,1)} %param.7) | copy-start | bytes 239620
  61.9 295.4 %copy-start.4 = (bf16[512,832]{0,1:T(8,128)(2,1)S(1)}, bf16[512,832]{0,1:T(8,128)(2,1)}, u32[]{:S(2)}) copy-start(bf16[512,832]{0,1:T(8,128)(2,1)} %param.10) | copy-start | bytes 2555908
  62.0 295.4 %all-gather.7.cloned.1.call-start = ((), (), s32[]{:S(2)}) async-start(), calls=%async_computation.4 | async-start | bytes 2838528 | tf_op jit(solution)/shard_map/all_gather | solution.py:33
  272.3 170.3 %all-gather.9.cloned.1.call-start = ((), (), s32[]{:S(2)}) async-start(), calls=%async_computation.5 | async-start | bytes 2838528 | tf_op jit(solution)/shard_map/all_gather | solution.py:34
  272.9 255.5 %all-gather.11.cloned.1.call-start = ((), (), s32[]{:S(2)}) async-start(), calls=%async_computation.7 | async-start | bytes 2838528 | tf_op jit(solution)/shard_map/all_gather | solution.py:32
  273.5 169.1 %copy-start.5 = (bf16[512,832]{0,1:T(8,128)(2,1)S(1)}, bf16[512,832]{0,1:T(8,128)(2,1)}, u32[]{:S(2)}) copy-start(bf16[512,832]{0,1:T(8,128)(2,1)} %param.11) | copy-start | bytes 2555908
  273.5 319.7 %reduce-scatter.5.cloned.1.call-start = ((), (), s32[]{:S(2)}) async-start(), calls=%async_computation.6 | async-start | bytes 1671168 | tf_op jit(solution)/shard_map/reduce_scatter | solution.py:42
  362.6 165.9 %copy-start.3 = (bf16[1536,512]{1,0:T(8,128)(2,1)S(1)}, bf16[1536,512]{1,0:T(8,128)(2,1)}, u32[]{:S(2)}) copy-start(bf16[1536,512]{1,0:T(8,128)(2,1)} %all-gather.5.cloned.1.call-done) | copy-start | bytes 4718596
Sparse Core Ops, SparseCore 0:
  10.1 46.9 all-gather.4
  62.1 208.5 reduce-scatter.2
  274.9 82.4 all-gather.6
  360.9 81.7 all-gather.8
  446.7 81.7 all-gather.10
  531.9 61.1 reduce-scatter.4
where the time goes:
time: 600 us
  waiting for transfers between devices  564 us (94%)
  matrix products  19.9 us (3%)
  between operations  14.1 us (2%)
    reduce_scatter x1, waiting for transfers between devices, on_device(): lax.psum_scatter(lax.dot_general(grad_rows, down_weight, (((1,), (1,)), (...  209 us
    all_gather x1, waiting for transfers between devices, on_device(): lax.all_gather(gate_grad, 'col', axis=0, tiled=True)  83.8 us
    all_gather x1, waiting for transfers between devices, on_device(): lax.all_gather(hidden, 'col', axis=0, tiled=True)  80.1 us
    all_gather x1, waiting for transfers between devices, on_device(): lax.all_gather(up_grad, 'col', axis=0, tiled=True)  80 us
    reduce_scatter x1, waiting for transfers between devices, on_device(): lax.psum_scatter((summed + lax.dot_general(up_grad, up_weight, (((1,), (1...  60.5 us
    all_gather x1, waiting for transfers between devices, on_device(): grad_rows = lax.all_gather(grad_out, 'row', axis=0, tiled=True)  49.2 us
  transfers between devices with their start and end apart: 6, of which 6 were waited for; matrix products, arithmetic and copies ran while one was open for 3% of the time, Pallas kernels for 0%

commit v1 on v0

v1 whole, which is shorter than its diff:
```python
import functools

import jax
import jax.numpy as jnp
from jax import lax
from jax.experimental import pallas as pl
from jax.experimental.pallas import tpu as pltpu
from jax.sharding import PartitionSpec as P

NZ, NY, NX = 8, 8, 4
TOK = 48
PAIR = 96
UNITS = 832
WIDE = 2 * UNITS
HEAD = 768
FEAT = 512
MESH = pl.DeviceIdType.MESH
F32, BF16 = jnp.float32, jnp.bfloat16


def wrap(value, size):
    return lax.rem(value + 2 * size, size)


class Tree:
    def __init__(self, first, z2, y, x):
        self.first = first
        self.row = z2
        self.na, self.nb = (NY, NX) if first == "y" else (NX, NY)
        self.a, self.b = (y, x) if first == "y" else (x, y)
        self.la, self.lb = self.na // 2, self.nb // 2

    def offsets(self, dist):
        if dist == 0:
            return [0]
        if dist == self.la:
            return [dist]
        return [dist, -dist]

    def sign_b(self, d, side):
        sign = 1 if d % 2 == 0 else -1
        return sign if side == 0 else -sign

    def len_a(self, side):
        return self.la - side

    def len_b(self, side):
        return self.lb - side

    def at_a(self, off):
        return wrap(self.a + off, self.na)

    def at_b(self, off):
        return wrap(self.b + off, self.nb)

    def yx(self, off_a, off_b):
        ia, ib = self.at_a(off_a), self.at_b(off_b)
        return (ia, ib) if self.first == "y" else (ib, ia)

    def device(self, off_a, off_b):
        iy, ix = self.yx(off_a, off_b)
        return (self.row, iy * NX + ix)


def side_of(d):
    return 0 if d > 0 else 1


class Gather:
    def __init__(self, tree, buf, s1, r1, s2, r2):
        self.t, self.buf = tree, buf
        self.s1, self.r1, self.s2, self.r2 = s1, r1, s2, r2

    def copy_a(self, side, hop):
        t = self.t
        sgn = 1 - 2 * side
        iy, ix = t.yx(-sgn * (hop - 1), 0)
        ref = self.buf.at[iy, ix]
        return pltpu.make_async_remote_copy(
            src_ref=ref, dst_ref=ref, send_sem=self.s1.at[side, hop - 1], recv_sem=self.r1.at[side, hop - 1],
            device_id=t.device(sgn, 0), device_id_type=MESH)

    def copy_b(self, d, side, hop):
        t = self.t
        sgn = t.sign_b(d, side)
        iy, ix = t.yx(-d, -sgn * (hop - 1))
        ref = self.buf.at[iy, ix]
        return pltpu.make_async_remote_copy(
            src_ref=ref, dst_ref=ref, send_sem=self.s2.at[side, hop - 1, d + 3], recv_sem=self.r2.at[side, hop - 1, d + 3],
            device_id=t.device(0, sgn), device_id_type=MESH)

    def recv_a(self, side, hop):
        sgn = 1 - 2 * side
        iy, ix = self.t.yx(-sgn * hop, 0)
        ref = self.buf.at[iy, ix]
        pltpu.make_async_remote_copy(
            src_ref=ref, dst_ref=ref, send_sem=self.s1.at[side, hop - 1], recv_sem=self.r1.at[side, hop - 1],
            device_id=self.t.device(-sgn, 0), device_id_type=MESH).wait_recv()

    def recv_b(self, d, side, hop):
        sgn = self.t.sign_b(d, side)
        iy, ix = self.t.yx(-d, -sgn * hop)
        ref = self.buf.at[iy, ix]
        pltpu.make_async_remote_copy(
            src_ref=ref, dst_ref=ref, send_sem=self.s2.at[side, hop - 1, d + 3], recv_sem=self.r2.at[side, hop - 1, d + 3],
            device_id=self.t.device(0, -sgn), device_id_type=MESH).wait_recv()

    def open_column(self, d):
        for side in (0, 1):
            self.copy_b(d, side, 1).start()

    def begin(self):
        self.copy_a(0, 1).start()
        self.copy_a(1, 1).start()
        self.open_column(0)

    def leaf(self, side, hop):
        return hop == self.t.len_b(side)

    def step(self, time):
        t = self.t
        for side in (0, 1):
            if time <= t.len_a(side):
                self.recv_a(side, time)
                if time < t.len_a(side):
                    self.copy_a(side, time + 1).start()
                self.open_column(time if side == 0 else -time)
        for hop in range(1, t.lb + 1):
            dist = time - hop
            if 0 <= dist <= t.la:
                for d in t.offsets(dist):
                    for side in (0, 1):
                        if hop < t.len_b(side):
                            self.recv_b(d, side, hop)
                            self.copy_b(d, side, hop + 1).start()

    def steps(self):
        return self.t.la + self.t.lb

    def all_d(self):
        return [d for dist in range(self.t.la + 1) for d in self.t.offsets(dist)]

    def leaves(self, d):
        for side in (0, 1):
            self.recv_b(d, side, self.t.len_b(side))

    def drain(self):
        for side in (0, 1):
            for hop in range(1, self.t.len_a(side) + 1):
                self.copy_a(side, hop).wait_send()
        for d in self.all_d():
            for side in (0, 1):
                for hop in range(1, self.t.len_b(side) + 1):
                    self.copy_b(d, side, hop).wait_send()


class Scatter:
    def __init__(self, tree, part, out1, in1, out2, in2, s1, r1, s2, r2):
        self.t, self.part = tree, part
        self.out1, self.in1, self.out2, self.in2 = out1, in1, out2, in2
        self.s1, self.r1, self.s2, self.r2 = s1, r1, s2, r2

    def copy_b(self, d, side, hop):
        t = self.t
        sgn = t.sign_b(d, side)
        if hop == t.len_b(side):
            iy, ix = t.yx(-d, -sgn * hop)
            src = self.part.at[iy, ix]
        else:
            src = self.out2.at[side, hop - 1, d + 3]
        return pltpu.make_async_remote_copy(
            src_ref=src, dst_ref=self.in2.at[side, hop - 1, d + 3], send_sem=self.s2.at[side, hop - 1, d + 3],
            recv_sem=self.r2.at[side, hop - 1, d + 3], device_id=t.device(0, -sgn), device_id_type=MESH)

    def copy_a(self, side, hop):
        t = self.t
        sgn = 1 - 2 * side
        return pltpu.make_async_remote_copy(
            src_ref=self.out1.at[side, hop - 1], dst_ref=self.in1.at[side, hop - 1], send_sem=self.s1.at[side, hop - 1],
            recv_sem=self.r1.at[side, hop - 1], device_id=t.device(-sgn, 0), device_id_type=MESH)

    def got_b(self, d, side, hop):
        sgn = self.t.sign_b(d, side)
        ref = self.in2.at[side, hop - 1, d + 3]
        pltpu.make_async_remote_copy(
            src_ref=ref, dst_ref=ref, send_sem=self.s2.at[side, hop - 1, d + 3], recv_sem=self.r2.at[side, hop - 1, d + 3],
            device_id=self.t.device(0, sgn), device_id_type=MESH).wait_recv()
        return ref

    def got_a(self, side, hop):
        sgn = 1 - 2 * side
        ref = self.in1.at[side, hop - 1]
        pltpu.make_async_remote_copy(
            src_ref=ref, dst_ref=ref, send_sem=self.s1.at[side, hop - 1], recv_sem=self.r1.at[side, hop - 1],
            device_id=self.t.device(sgn, 0), device_id_type=MESH).wait_recv()
        return ref

    def send_b(self, d, side, hop):
        t = self.t
        if hop < t.len_b(side):
            got = self.got_b(d, side, hop + 1)
            iy, ix = t.yx(-d, -t.sign_b(d, side) * hop)
            self.out2[side, hop - 1, d + 3] = (self.part[iy, ix].astype(F32) + got[...].astype(F32)).astype(BF16)
        self.copy_b(d, side, hop).start()

    def column_sum(self, d):
        one, two = self.got_b(d, 0, 1), self.got_b(d, 1, 1)
        iy, ix = self.t.yx(-d, 0)
        return self.part[iy, ix].astype(F32) + one[...].astype(F32) + two[...].astype(F32)

    def send_a(self, side, hop):
        t = self.t
        total = self.column_sum(hop if side == 0 else -hop)
        if hop < t.len_a(side):
            total = total + self.got_a(side, hop + 1)[...].astype(F32)
        self.out1[side, hop - 1] = total.astype(BF16)
        self.copy_a(side, hop).start()

    def events(self, depth):
        t = self.t
        leaves, inner = [], []
        for hop in range(t.lb, 0, -1):
            dist = depth - hop
            if 0 <= dist <= t.la:
                for d in t.offsets(dist):
                    for side in (0, 1):
                        if hop == t.len_b(side):
                            leaves.append((d, side, hop))
                        elif hop < t.len_b(side):
                            inner.append((d, side, hop))
        return leaves, inner

    def step(self, depth, ahead=2):
        t = self.t
        top = t.la + t.lb
        depths = range(top, top - ahead - 1, -1) if depth == top else [depth - ahead]
        for later in depths:
            if later >= 1:
                for event in self.events(later)[0]:
                    self.send_b(*event)
        for side in (0, 1):
            if depth <= t.len_a(side):
                self.send_a(side, depth)
        for event in self.events(depth)[1]:
            self.send_b(*event)

    def result(self):
        return self.column_sum(0) + self.got_a(0, 1)[...].astype(F32) + self.got_a(1, 1)[...].astype(F32)

    def drain(self):
        t = self.t
        for side in (0, 1):
            for hop in range(1, t.len_a(side) + 1):
                self.copy_a(side, hop).wait_send()
        for dist in range(t.la + 1):
            for d in t.offsets(dist):
                for side in (0, 1):
                    for hop in range(1, t.len_b(side) + 1):
                        self.copy_b(d, side, hop).wait_send()


def nt_dot(left, right):
    return lax.dot_general(left, right, (((1,), (1,)), ((), ())), preferred_element_type=F32)


def kernel(grad_ref, gate_ref, up_ref, down_ref, gw_ref, uw_ref, in_grad_ref, down_grad_ref,
           rows, hid, part, gu, wcat, rs_out1, rs_in1, rs_out2, rs_in2, hg,
           pair_out, pair_in, z_out, z_in, own,
           h_s1, h_r1, h_s2, h_r2, g_s1, g_r1, g_s2, g_r2, p_s1, p_r1, p_s2, p_r2,
           za_s, za_r, zc_s, zc_r, pair_s, pair_r, zs_s, zs_r):
    row, col = lax.axis_index("row"), lax.axis_index("col")
    z, core = row // 2, lax.rem(row, 2)
    y, x = col // NX, lax.rem(col, NX)
    other = 1 - core
    z_at = lambda off: wrap(z + off, NZ)
    y_at = lambda off: wrap(y + off, NY)
    sibling = (z * 2 + other, col)

    trees = (Tree("y", row, y, x), Tree("x", row, y, x))

    def per_core(fn):
        for which in (0, 1):
            pl.when(core == which)(functools.partial(fn, trees[which]))

    def barrier_partners():
        yield sibling
        for off in range(1, NZ):
            yield (z_at(off) * 2 + core, col)
        for off in (1, -1):
            yield (row, y_at(off) * NX + x)
            yield (row, y * NX + wrap(x + off, NX))

    barrier = pltpu.get_barrier_semaphore()
    count = 0
    for partner in barrier_partners():
        pl.semaphore_signal(barrier, inc=1, device_id=partner, device_id_type=MESH)
        count += 1

    gate = gate_ref[...].astype(F32)
    sig = jax.nn.sigmoid(gate)
    hid[y, x] = (gate * sig * up_ref[...].astype(F32)).astype(BF16)
    rows[row] = grad_ref[...]
    pl.semaphore_wait(barrier, count)

    def z_copy(side, hop):
        sgn = 1 - 2 * side
        ref = rows.at[z_at(-sgn * (hop - 1)) * 2 + core]
        return pltpu.make_async_remote_copy(
            src_ref=ref, dst_ref=ref, send_sem=za_s.at[side, hop - 1], recv_sem=za_r.at[side, hop - 1],
            device_id=(z_at(sgn) * 2 + core, col), device_id_type=MESH)

    def z_recv(side, hop):
        sgn = 1 - 2 * side
        ref = rows.at[z_at(-sgn * hop) * 2 + core]
        pltpu.make_async_remote_copy(
            src_ref=ref, dst_ref=ref, send_sem=za_s.at[side, hop - 1], recv_sem=za_r.at[side, hop - 1],
            device_id=(z_at(-sgn) * 2 + core, col), device_id_type=MESH).wait_recv()

    def cross_copy(off, which):
        ref = rows.at[z_at(off) * 2 + which]
        return pltpu.make_async_remote_copy(
            src_ref=ref, dst_ref=ref, send_sem=zc_s.at[off + 3], recv_sem=zc_r.at[off + 3],
            device_id=sibling, device_id_type=MESH)

    def hidden_gather(tree):
        return Gather(tree, hid, h_s1, h_r1, h_s2, h_r2)

    def grads_gather(tree):
        return Gather(tree, gu, g_s1, g_r1, g_s2, g_r2)

    def scatter(tree):
        return Scatter(tree, part, rs_out1, rs_in1, rs_out2, rs_in2, p_s1, p_r1, p_s2, p_r2)

    z_copy(0, 1).start()
    z_copy(1, 1).start()
    per_core(lambda tree: hidden_gather(tree).begin())
    cross_copy(0, core).start()
    wcat[:, :HEAD] = gw_ref[:, :HEAD]
    wcat[:, HEAD:2 * HEAD] = uw_ref[:, :HEAD]
    wcat[:, 2 * HEAD:] = jnp.concatenate([gw_ref[:, HEAD:], uw_ref[:, HEAD:]], axis=1)

    def matmul1(off):
        iz = z_at(off)
        block = rows[pl.ds(iz * 2, 2)].reshape(2 * PAIR, FEAT)
        part[iz] = nt_dot(block, down_ref[...]).astype(BF16).reshape(NX, TOK, UNITS)

    for hop in range(1, NZ // 2 + 1):
        for side in (0, 1):
            if hop <= NZ // 2 - side:
                z_recv(side, hop)
                if hop < NZ // 2 - side:
                    z_copy(side, hop + 1).start()
                cross_copy(-hop if side == 0 and hop < 4 else hop, core).start()
        per_core(lambda tree: hidden_gather(tree).step(hop))
    offs = [0, -1, 1, -2, 2, -3, 3, 4]
    for off in offs:
        cross_copy(off, other).wait_recv()
        matmul1(off)
    for time in (5, 6):
        per_core(lambda tree: hidden_gather(tree).step(time))

    for depth in range(6, 0, -1):
        per_core(lambda tree: scatter(tree).step(depth))

    def finish(tree):
        hg[...] = scatter(tree).result()

    per_core(finish)
    grad = hg[...]
    upv = up_ref[...].astype(F32)
    ug = (grad * (gate * sig)).astype(BF16)
    gg = (grad * upv * sig * (1.0 + gate * (1.0 - sig))).astype(BF16)
    gu[y, x, :, :HEAD] = gg[:, :HEAD]
    gu[y, x, :, HEAD:2 * HEAD] = ug[:, :HEAD]
    gu[y, x, :, 2 * HEAD:] = jnp.concatenate([gg[:, HEAD:], ug[:, HEAD:]], axis=1)

    per_core(lambda tree: grads_gather(tree).begin())

    def hidden_leaves(tree):
        gather = hidden_gather(tree)
        for d in gather.all_d():
            gather.leaves(d)

    per_core(hidden_leaves)
    all_rows = rows[...].reshape(NZ * 2 * PAIR, FEAT)
    for start, size in ((0, 256), (256, 256), (512, 320)):
        units = hid[:, :, :, pl.ds(start, size)].reshape(NY * NX * TOK, size)
        down_grad_ref[pl.ds(start, size)] = lax.dot_general(
            units, all_rows, (((0,), (0,)), ((), ())), preferred_element_type=F32).astype(BF16)

    def pair_copy(off):
        return pltpu.make_async_remote_copy(
            src_ref=pair_out.at[off + 3], dst_ref=pair_in.at[off + 3], send_sem=pair_s.at[off + 3],
            recv_sem=pair_r.at[off + 3], device_id=sibling, device_id_type=MESH)

    def z_send(off):
        return pltpu.make_async_remote_copy(
            src_ref=z_out.at[off + 3], dst_ref=z_in.at[z], send_sem=zs_s.at[off + 3], recv_sem=zs_r.at[z],
            device_id=(y_at(off) * 2 + core, col), device_id_type=MESH)

    def block_leaves(tree, off):
        gather = grads_gather(tree)
        if tree.first == "y":
            gather.leaves(-off if off != 4 else 4)
        else:
            for d in gather.all_d():
                for side in (0, 1):
                    sgn = tree.sign_b(d, side)
                    hop = abs(off)
                    if hop == tree.len_b(side) and (-sgn * hop - off) % NY == 0:
                        gather.recv_b(d, side, hop)

    def block(off):
        per_core(lambda tree: block_leaves(tree, off))
        iy = y_at(off)
        both = gu[iy].reshape(NX * TOK, WIDE)
        total = nt_dot(both, wcat[...])
        lower, upper = total[:PAIR], total[PAIR:]
        mine = jnp.where(core == 0, lower, upper)
        theirs = jnp.where(core == 0, upper, lower)
        pair_out[off + 3] = theirs.astype(BF16)
        own[off + 3] = mine
        pair_copy(off).start()

    def pass_on(off):
        pair_copy(off).wait_recv()
        total = own[off + 3] + pair_in[off + 3].astype(F32)
        own[off + 3] = total

        @pl.when(y_at(off) != z)
        def _():
            z_out[off + 3] = total.astype(BF16)
            z_send(off).start()

        @pl.when(y_at(off) == z)
        def _():
            own[8] = total

    done = []

    def run_block(off):
        block(off)
        if done:
            pass_on(done[-1])
        done.append(off)

    for time in range(1, 7):
        per_core(lambda tree: grads_gather(tree).step(time))
        dist = time - 3
        if dist >= 0:
            for off in ([0] if dist == 0 else [dist, -dist]):
                run_block(off)
    run_block(4)
    pass_on(4)

    total = own[8]
    for off in range(1, NZ):
        iz = z_at(off)
        ref = z_in.at[iz]
        pltpu.make_async_remote_copy(
            src_ref=ref, dst_ref=ref, send_sem=zs_s.at[0], recv_sem=zs_r.at[iz],
            device_id=(iz * 2 + core, col), device_id_type=MESH).wait_recv()
        total = total + ref[...].astype(F32)
    in_grad_ref[...] = total.astype(BF16)

    for side in (0, 1):
        for hop in range(1, NZ // 2 + 1 - side):
            z_copy(side, hop).wait_send()
    for off in range(-3, 5):
        cross_copy(off, core).wait_send()
        pair_copy(off).wait_send()
        pl.when(y_at(off) != z)(lambda: z_send(off).wait_send())

    def drain(tree):
        hidden_gather(tree).drain()
        scatter(tree).drain()
        grads_gather(tree).drain()

    per_core(drain)


def on_device(grad_out, gate_pre, up_pre, down_weight, gate_weight, up_weight):
    vmem = pl.BlockSpec(memory_space=pltpu.VMEM)
    dma = pltpu.SemaphoreType.DMA
    tree_sems = [dma((2, 4)), dma((2, 4)), dma((2, 4, 8)), dma((2, 4, 8))]
    return pl.pallas_call(
        kernel,
        out_shape=(
            jax.ShapeDtypeStruct((PAIR, FEAT), BF16),
            jax.ShapeDtypeStruct((UNITS, FEAT), BF16),
        ),
        in_specs=[vmem] * 6,
        out_specs=(vmem, vmem),
        scratch_shapes=[
            pltpu.VMEM((2 * NZ, PAIR, FEAT), BF16),
            pltpu.VMEM((NY, NX, TOK, UNITS), BF16),
            pltpu.VMEM((NY, NX, TOK, UNITS), BF16),
            pltpu.VMEM((NY, NX, TOK, WIDE), BF16),
            pltpu.VMEM((FEAT, WIDE), BF16),
            pltpu.VMEM((2, 4, TOK, UNITS), BF16),
            pltpu.VMEM((2, 4, TOK, UNITS), BF16),
            pltpu.VMEM((2, 4, 8, TOK, UNITS), BF16),
            pltpu.VMEM((2, 4, 8, TOK, UNITS), BF16),
            pltpu.VMEM((TOK, UNITS), F32),
            pltpu.VMEM((8, PAIR, FEAT), BF16),
            pltpu.VMEM((8, PAIR, FEAT), BF16),
            pltpu.VMEM((8, PAIR, FEAT), BF16),
            pltpu.VMEM((8, PAIR, FEAT), BF16),
            pltpu.VMEM((9, PAIR, FEAT), F32),
        ] + tree_sems * 3 + [dma((2, 4)), dma((2, 4))] + [dma((8,))] * 6,
        compiler_params=pltpu.CompilerParams(
            collective_id=0, has_side_effects=True, vmem_limit_bytes=56 * 2**20),
        cost_estimate=pl.CostEstimate(flops=5_234_491_392, bytes_accessed=4_000_000, transcendentals=40_000),
    )(grad_out, gate_pre, up_pre, down_weight, gate_weight, up_weight)


def solution(mesh):
    placed = (
        P("row", "col"),
        P("col", "row"),
        P("col", "row"),
        P("row", "col"),
        P("col", "row"),
        P("col", "row"),
    )
    return jax.shard_map(
        on_device,
        mesh=mesh,
        in_specs=placed,
        out_specs=(P("row", "col"), P("row", "col")),
        check_vma=False,
    )
```

time: 600 us -> 133 us (0.22)
  the two profiles are of different devices: /device:TPU:18 before, /device:TPU:30 now
where the time goes in v1:
time: 133 us; the launch traced here: 132 us
  Pallas kernels  125 us (94%)
  local copies, waits for them, and re-layouts  7.22 us (5%)
    pallas_call x1, Pallas kernels, on_device(): pl.pallas_call(kernel, out_shape=(jax.ShapeDtypeStruct((PAIR, FEAT), BF16...  125 us
    unnamed x6, local copies, waits for them, and re-layouts  7.22 us

profile of v1, /device:TPU:30, one launch (start us, length us, event | category | flops | bytes accessed | tf_op | source)
XLA Modules:
  0.0 132.4 jit_solution(9292760838556960820)
XLA Ops:
  0.6 0.0 copy-start
  0.6 2.3 %copy.8.gw_ref = bf16[512,832]{1,0:T(8,128)(2,1)} copy(bf16[512,832]{0,1:T(8,128)(2,1)} %param.10) | data formatting | bytes 1703936 | tf_op args[4]
  2.9 0.0 copy-done
  2.9 1.3 copy.9.uw_ref
  4.2 124.5 %shard_map.77 = (bf16[96,512]{1,0:T(8,128)(2,1)}, bf16[832,512]{1,0:T(8,128)(2,1)}) custom-call(bf16[96,512]{1,0:T(8,128)(2,1)} %grad_ref.1, bf16[48,832]{1,0:T(8,128)(2,1)} %gate_ref.1, bf16[48,832]{1,0:T(8,128)(2,1)} %up_ref.1, bf16[832,512]{1,0:T(8,128)(2,1)} %down_ref.1, bf16[512,832]{1,0:T(8,128)(2,1)} %copy.8.gw_ref, bf16[512,832]{1,0:T(8,128)(2,1)} %copy.9.uw_ref), custom_call_target="tpu_custom_call" | custom-call | flops 5234491392 | bytes 4000000 | tf_op jit(solution)/shard_map/pallas_call | solution.py:486
  128.7 1.5 %copy.12 = bf16[96,512]{1,0:T(8,128)(2,1)} copy(bf16[96,512]{1,0:T(8,128)(2,1)} %get-tuple-element.4) | data formatting | bytes 196608
  130.3 2.1 %copy.13 = bf16[832,512]{1,0:T(8,128)(2,1)} copy(bf16[832,512]{1,0:T(8,128)(2,1)} %get-tuple-element.5) | data formatting | bytes 1703936
Async XLA Ops:
  0.6 2.3 %copy-start = (bf16[512,832]{0,1:T(8,128)(2,1)S(1)}, bf16[512,832]{0,1:T(8,128)(2,1)}, u32[]{:S(2)}) copy-start(bf16[512,832]{0,1:T(8,128)(2,1)} %param.11) | copy-start | bytes 2555908

commit v2 on v0

v2 whole, which is shorter than its diff:
```python
import functools

import jax
import jax.numpy as jnp
from jax import lax
from jax.experimental import pallas as pl
from jax.experimental.pallas import tpu as pltpu
from jax.sharding import PartitionSpec as P

NZ, NY, NX = 8, 8, 4
TOK = 48
PAIR = 96
UNITS = 832
WIDE = 2 * UNITS
HEAD = 768
FEAT = 512
MESH = pl.DeviceIdType.MESH
F32, BF16 = jnp.float32, jnp.bfloat16


def wrap(value, size):
    return lax.rem(value + 2 * size, size)


class Torus:
    def __init__(self, row, y, x):
        self.row, self.y, self.x = row, y, x

    def yx(self, off_y, off_x):
        return wrap(self.y + off_y, NY), wrap(self.x + off_x, NX)

    def device(self, off_y, off_x):
        iy, ix = self.yx(off_y, off_x)
        return (self.row, iy * NX + ix)


LONG = NY // 2
HOPS = (LONG, LONG - 1)
DIRECT = (2, 1, -1)
COLUMNS = (0, 1, -1, 2)


def y_offsets(dist):
    return [dist] if dist in (0, LONG) else [dist, -dist]


FAR_FIRST = [d for dist in range(LONG, -1, -1) for d in y_offsets(dist)]


def sign(d, side):
    return 1 - 2 * ((d + side) % 2)


def chain_slot(d, side, hop):
    return (side * LONG + hop - 1) * 4 + d + 1


def direct_slot(d, e):
    return DIRECT.index(e) * 8 + d + 3


def remote(src, dst, send, recv, device):
    return pltpu.make_async_remote_copy(
        src_ref=src, dst_ref=dst, send_sem=send, recv_sem=recv, device_id=device, device_id_type=MESH)


class GatherYX:
    def __init__(self, t, buf, s1, r1, s2, r2):
        self.t, self.buf, self.s1, self.r1, self.s2, self.r2 = t, buf, s1, r1, s2, r2

    def ref(self, off_y, off_x):
        return self.buf.at[self.t.yx(off_y, off_x)]

    def copy_y(self, side, hop, to=0):
        sgn = 1 - 2 * side
        ref = self.ref(-sgn * (hop - 1 + to), 0)
        slot = side * LONG + hop - 1
        return remote(ref, ref, self.s1.at[slot], self.r1.at[slot], self.t.device(sgn, 0))

    def copy_x(self, d, e, to=0):
        ref = self.ref(-d, -e * to)
        slot = direct_slot(d, e)
        return remote(ref, ref, self.s2.at[slot], self.r2.at[slot], self.t.device(0, e))

    def open(self, d):
        for e in DIRECT:
            self.copy_x(d, e).start()

    def begin(self):
        for side in (0, 1):
            self.copy_y(side, 1).start()
        self.open(0)

    def step(self, time):
        for side in (0, 1):
            if time <= HOPS[side]:
                self.copy_y(side, time, 1).wait_recv()
                if time < HOPS[side]:
                    self.copy_y(side, time + 1).start()
        for side in (0, 1):
            if time <= HOPS[side]:
                self.open(time if side == 0 else -time)

    def leaves(self, off):
        for e in DIRECT:
            self.copy_x(off if off == LONG else -off, e, 1).wait_recv()

    def drain(self):
        for side in (0, 1):
            for hop in range(1, HOPS[side] + 1):
                self.copy_y(side, hop).wait_send()
        for d in FAR_FIRST:
            for e in DIRECT:
                self.copy_x(d, e).wait_send()


class GatherXY:
    def __init__(self, t, buf, s1, r1, s2, r2):
        self.t, self.buf, self.s1, self.r1, self.s2, self.r2 = t, buf, s1, r1, s2, r2

    def ref(self, off_y, off_x):
        return self.buf.at[self.t.yx(off_y, off_x)]

    def copy_x(self, e, to=0):
        ref = self.ref(0, -e * to)
        slot = DIRECT.index(e)
        return remote(ref, ref, self.s1.at[slot], self.r1.at[slot], self.t.device(0, e))

    def copy_y(self, d, side, hop, to=0):
        sgn = sign(d, side)
        ref = self.ref(-sgn * (hop - 1 + to), -d)
        slot = chain_slot(d, side, hop)
        return remote(ref, ref, self.s2.at[slot], self.r2.at[slot], self.t.device(sgn, 0))

    def begin(self):
        for e in DIRECT:
            self.copy_x(e).start()
        for side in (0, 1):
            self.copy_y(0, side, 1).start()

    def step(self, time):
        if time == 1:
            for e in (1, -1, 2):
                self.copy_x(e, 1).wait_recv()
                for side in (0, 1):
                    self.copy_y(e, side, 1).start()
        for d in COLUMNS:
            hop = time if d == 0 else time - 1
            for side in (0, 1):
                if 1 <= hop < HOPS[side]:
                    self.copy_y(d, side, hop, 1).wait_recv()
                    self.copy_y(d, side, hop + 1).start()

    def leaves(self, off):
        for d in COLUMNS:
            for side in (0, 1):
                hop = HOPS[side]
                if hop == abs(off) and (-sign(d, side) * hop - off) % NY == 0:
                    self.copy_y(d, side, hop, 1).wait_recv()

    def drain(self):
        for e in DIRECT:
            self.copy_x(e).wait_send()
        for d in COLUMNS:
            for side in (0, 1):
                for hop in range(1, HOPS[side] + 1):
                    self.copy_y(d, side, hop).wait_send()


class ScatterYX:
    def __init__(self, t, part, out1, in1, out2, in2, s1, r1, s2, r2):
        self.t, self.part, self.out1, self.in1, self.in2 = t, part, out1, in1, in2
        self.s1, self.r1, self.s2, self.r2 = s1, r1, s2, r2

    def copy_x(self, d, e):
        slot = direct_slot(d, e)
        return remote(self.part.at[self.t.yx(-d, -e)], self.in2.at[slot], self.s2.at[slot], self.r2.at[slot],
                      self.t.device(0, -e))

    def copy_y(self, side, hop):
        slot = side * LONG + hop - 1
        return remote(self.out1.at[slot], self.in1.at[slot], self.s1.at[slot], self.r1.at[slot],
                      self.t.device(-1 + 2 * side, 0))

    def open(self, d):
        for e in DIRECT:
            self.copy_x(d, e).start()

    def column_sum(self, d):
        total = self.part[self.t.yx(-d, 0)].astype(F32)
        for e in DIRECT:
            self.copy_x(d, e).wait_recv()
            total = total + self.in2[direct_slot(d, e)].astype(F32)
        return total

    def got_y(self, side, hop):
        self.copy_y(side, hop).wait_recv()
        return self.in1[side * LONG + hop - 1].astype(F32)

    def step(self, depth):
        for side in (0, 1):
            if depth <= HOPS[side]:
                total = self.column_sum(depth if side == 0 else -depth)
                if depth < HOPS[side]:
                    total = total + self.got_y(side, depth + 1)
                self.out1[side * LONG + depth - 1] = total.astype(BF16)
                self.copy_y(side, depth).start()

    def result(self):
        return self.column_sum(0) + self.got_y(0, 1) + self.got_y(1, 1)

    def drain(self):
        for side in (0, 1):
            for hop in range(1, HOPS[side] + 1):
                self.copy_y(side, hop).wait_send()
        for d in FAR_FIRST:
            for e in DIRECT:
                self.copy_x(d, e).wait_send()


class ScatterXY:
    def __init__(self, t, part, out1, in1, out2, in2, s1, r1, s2, r2):
        self.t, self.part, self.out1, self.in1, self.out2, self.in2 = t, part, out1, in1, out2, in2
        self.s1, self.r1, self.s2, self.r2 = s1, r1, s2, r2

    def copy_y(self, d, side, hop):
        sgn = sign(d, side)
        slot = chain_slot(d, side, hop)
        if hop == HOPS[side]:
            src = self.part.at[self.t.yx(-sgn * hop, -d)]
        else:
            src = self.out2.at[slot]
        return remote(src, self.in2.at[slot], self.s2.at[slot], self.r2.at[slot], self.t.device(-sgn, 0))

    def copy_x(self, e):
        slot = DIRECT.index(e)
        return remote(self.out1.at[slot], self.in1.at[slot], self.s1.at[slot], self.r1.at[slot], self.t.device(0, -e))

    def open(self, off):
        for d in (2, 1, -1, 0):
            for side in (0, 1):
                if HOPS[side] == abs(off) and (sign(d, side) * HOPS[side] - off) % NY == 0:
                    self.copy_y(d, side, HOPS[side]).start()

    def got_y(self, d, side, hop):
        self.copy_y(d, side, hop).wait_recv()
        return self.in2[chain_slot(d, side, hop)].astype(F32)

    def column_sum(self, d):
        return self.part[self.t.yx(0, -d)].astype(F32) + self.got_y(d, 0, 1) + self.got_y(d, 1, 1)

    def step(self, depth):
        for d in (2, 1, -1, 0):
            for side in (0, 1):
                hop = depth - 1
                if 1 <= hop < HOPS[side]:
                    total = self.part[self.t.yx(-sign(d, side) * hop, -d)].astype(F32) + self.got_y(d, side, hop + 1)
                    self.out2[chain_slot(d, side, hop)] = total.astype(BF16)
                    self.copy_y(d, side, hop).start()
            if depth == 1 and d != 0:
                self.out1[DIRECT.index(d)] = self.column_sum(d).astype(BF16)
                self.copy_x(d).start()

    def result(self):
        total = self.column_sum(0)
        for e in DIRECT:
            self.copy_x(e).wait_recv()
            total = total + self.in1[DIRECT.index(e)].astype(F32)
        return total

    def drain(self):
        for e in DIRECT:
            self.copy_x(e).wait_send()
        for d in COLUMNS:
            for side in (0, 1):
                for hop in range(1, HOPS[side] + 1):
                    self.copy_y(d, side, hop).wait_send()


def nt_dot(left, right):
    return lax.dot_general(left, right, (((1,), (1,)), ((), ())), preferred_element_type=F32)


def kernel(grad_ref, gate_ref, up_ref, down_hbm, gw_hbm, uw_hbm, in_grad_ref, down_grad_ref,
           rows, hid, part, gu, down_ref, wcat, rs_out1, rs_in1, rs_out2, rs_in2, hg,
           pair_out, pair_in, z_out, z_in, own,
           h_s1, h_r1, h_s2, h_r2, g_s1, g_r1, g_s2, g_r2, p_s1, p_r1, p_s2, p_r2,
           za_s, za_r, zc_s, zc_r, pair_s, pair_r, zs_s, zs_r, load_sem):
    row, col = lax.axis_index("row"), lax.axis_index("col")
    z, core = row // 2, lax.rem(row, 2)
    y, x = col // NX, lax.rem(col, NX)
    other = 1 - core
    way = 1 - 2 * core
    z_at = lambda off: wrap(z + off, NZ)
    y_at = lambda off: wrap(y + off, NY)
    sibling = (z * 2 + other, col)
    torus = Torus(row, y, x)

    def per_core(fn):
        for which in (0, 1):
            pl.when(core == which)(functools.partial(fn, which))

    partners = [sibling]
    partners += [(z_at(off) * 2 + core, col) for off in range(1, NZ)]
    partners += [torus.device(1, 0), torus.device(-1, 0)] + [torus.device(0, e) for e in DIRECT]
    barrier = pltpu.get_barrier_semaphore()
    for partner in partners:
        pl.semaphore_signal(barrier, inc=1, device_id=partner, device_id_type=MESH)

    loads = [pltpu.make_async_copy(down_hbm, down_ref, load_sem.at[0])]
    for i, (src, size, at) in enumerate(((gw_hbm, HEAD, 0), (uw_hbm, HEAD, HEAD))):
        loads.append(pltpu.make_async_copy(src.at[pl.ds(0, size)], wcat.at[pl.ds(at, size)], load_sem.at[1 + 2 * i]))
        loads.append(pltpu.make_async_copy(
            src.at[pl.ds(HEAD, UNITS - HEAD)], wcat.at[pl.ds(2 * HEAD + i * (UNITS - HEAD), UNITS - HEAD)],
            load_sem.at[2 + 2 * i]))
    for load in loads:
        load.start()

    gate = gate_ref[...].astype(F32)
    sig = jax.nn.sigmoid(gate)
    hid[y, x] = (gate * sig * up_ref[...].astype(F32)).astype(BF16)
    rows[row] = grad_ref[...]
    pl.semaphore_wait(barrier, len(partners))

    def z_copy(off, via=0, to=0):
        ref = rows.at[z_at(-way * (off if to else via)) * 2 + core]
        slot = off + 3
        return remote(ref, ref, za_s.at[slot], za_r.at[slot], (z_at(way * (off - via)) * 2 + core, col))

    def cross_copy(off, which):
        ref = rows.at[z_at(off) * 2 + which]
        return remote(ref, ref, zc_s.at[off + 3], zc_r.at[off + 3], sibling)

    def cross_slot(off, sgn):
        return 4 if abs(off) == 4 else off * sgn

    def hidden_gather(which):
        return (GatherYX, GatherXY)[which](torus, hid, h_s1, h_r1, h_s2, h_r2)

    def grads_gather(which):
        return (GatherYX, GatherXY)[which](torus, gu, g_s1, g_r1, g_s2, g_r2)

    def scatter(which):
        return (ScatterYX, ScatterXY)[which](torus, part, rs_out1, rs_in1, rs_out2, rs_in2, p_s1, p_r1, p_s2, p_r2)

    def z_got(off):
        z_copy(off, 0, 1).wait_recv()

    def z_pass(off):
        def send(which):
            cross_copy(cross_slot(-off, 1 - 2 * which), which).start()

        per_core(send)

    for off in (2, -2, 1, -1):
        z_copy(off).start()
    per_core(lambda which: hidden_gather(which).begin())
    cross_copy(0, core).start()
    z_got(2)
    z_copy(4, 2).start()
    z_copy(3, 2).start()
    z_got(-2)
    z_copy(-3, -2).start()
    for off in (2, -2):
        z_pass(off)
    for off in (1, -1):
        z_got(off)
        z_pass(off)
    for time in (1, 2):
        per_core(lambda which: hidden_gather(which).step(time))
    for off in (3, -3, 4):
        z_got(off)
        z_pass(off)
    for load in loads:
        load.wait()
    for off in range(-3, 5):
        cross_copy(off, other).wait_recv()

    def matmul1(off):
        iz = y_at(off)
        block = rows[pl.ds(iz * 2, 2)].reshape(2 * PAIR, FEAT)
        part[iz] = nt_dot(block, down_ref[...]).astype(BF16).reshape(NX, TOK, UNITS)

    for off in FAR_FIRST:
        matmul1(-off)
        per_core(lambda which: scatter(which).open(off))
    for depth in (4, 3, 2, 1):
        per_core(lambda which: scatter(which).step(depth))

    def finish(which):
        hg[...] = scatter(which).result()

    per_core(finish)
    grad = hg[...]
    upv = up_ref[...].astype(F32)
    ug = (grad * (gate * sig)).astype(BF16)
    gg = (grad * upv * sig * (1.0 + gate * (1.0 - sig))).astype(BF16)
    gu[y, x, :, :HEAD] = gg[:, :HEAD]
    gu[y, x, :, HEAD:2 * HEAD] = ug[:, :HEAD]
    gu[y, x, :, 2 * HEAD:] = jnp.concatenate([gg[:, HEAD:], ug[:, HEAD:]], axis=1)

    per_core(lambda which: grads_gather(which).begin())

    def pair_copy(off):
        slot = off + 3
        return remote(pair_out.at[slot], pair_in.at[slot], pair_s.at[slot], pair_r.at[slot], sibling)

    def z_send(off):
        return remote(z_out.at[off + 3], z_in.at[z], zs_s.at[off + 3], zs_r.at[z], (y_at(off) * 2 + core, col))

    def block(off):
        per_core(lambda which: grads_gather(which).leaves(off))
        both = gu[y_at(off)].reshape(NX * TOK, WIDE)
        total = jnp.dot(both, wcat[...], preferred_element_type=F32)
        lower, upper = total[:PAIR], total[PAIR:]
        own[off + 3] = jnp.where(core == 0, lower, upper)
        pair_out[off + 3] = jnp.where(core == 0, upper, lower).astype(BF16)
        pair_copy(off).start()

    def pass_on(off):
        pair_copy(off).wait_recv()
        total = own[off + 3] + pair_in[off + 3].astype(F32)

        @pl.when(y_at(off) != z)
        def _():
            z_out[off + 3] = total.astype(BF16)
            z_send(off).start()

        @pl.when(y_at(off) == z)
        def _():
            own[8] = total

    for time in (1, 2, 3, 4):
        per_core(lambda which: grads_gather(which).step(time))
        if time == 2:
            block(0)
        if time == 3:
            pass_on(0)
            block(1)
            block(-1)
    pass_on(1)
    pass_on(-1)
    for time in (3, 4):
        per_core(lambda which: hidden_gather(which).step(time))
    for off in (2, -2):
        block(off)
    for off in (2, -2):
        pass_on(off)
    for off in (3, -3):
        block(off)
    for off in (3, -3):
        pass_on(off)
    block(4)
    pass_on(4)

    def hidden_leaves(which):
        for off in FAR_FIRST:
            hidden_gather(which).leaves(off)

    per_core(hidden_leaves)
    all_rows = rows[...].reshape(NZ * 2 * PAIR, FEAT)
    for start, size in ((0, 256), (256, 256), (512, 320)):
        units = hid[:, :, :, pl.ds(start, size)].reshape(NY * NX * TOK, size)
        down_grad_ref[pl.ds(start, size)] = lax.dot_general(
            units, all_rows, (((0,), (0,)), ((), ())), preferred_element_type=F32).astype(BF16)

    total = own[8]
    for off in range(1, NZ):
        iz = z_at(off)
        ref = z_in.at[iz]
        remote(ref, ref, zs_s.at[0], zs_r.at[iz], (iz * 2 + core, col)).wait_recv()
        total = total + ref[...].astype(F32)
    in_grad_ref[...] = total.astype(BF16)

    for off, via in ((2, 0), (-2, 0), (1, 0), (-1, 0), (4, 2), (3, 2), (-3, -2)):
        z_copy(off, via).wait_send()
    for off in range(-3, 5):
        cross_copy(off, core).wait_send()
        pair_copy(off).wait_send()
        pl.when(y_at(off) != z)(lambda: z_send(off).wait_send())

    def drain(which):
        hidden_gather(which).drain()
        scatter(which).drain()
        grads_gather(which).drain()

    per_core(drain)


def copy_out(a_ref, b_ref, a_out, b_out):
    a_out[...] = a_ref[...]
    b_out[...] = b_ref[...]


def on_device(grad_out, gate_pre, up_pre, down_weight, gate_weight, up_weight):
    vmem, anywhere = pl.BlockSpec(memory_space=pltpu.VMEM), pl.BlockSpec(memory_space=pl.ANY)
    dma = pltpu.SemaphoreType.DMA
    tree_sems = [dma((8,)), dma((8,)), dma((32,)), dma((32,))]
    outs = (jax.ShapeDtypeStruct((PAIR, FEAT), BF16), jax.ShapeDtypeStruct((UNITS, FEAT), BF16))
    input_grad, down_grad = pl.pallas_call(
        kernel,
        out_shape=outs,
        in_specs=[vmem] * 3 + [anywhere] * 3,
        out_specs=(vmem, vmem),
        scratch_shapes=[
            pltpu.VMEM((2 * NZ, PAIR, FEAT), BF16),
            pltpu.VMEM((NY, NX, TOK, UNITS), BF16),
            pltpu.VMEM((NY, NX, TOK, UNITS), BF16),
            pltpu.VMEM((NY, NX, TOK, WIDE), BF16),
            pltpu.VMEM((UNITS, FEAT), BF16),
            pltpu.VMEM((WIDE, FEAT), BF16),
            pltpu.VMEM((8, TOK, UNITS), BF16),
            pltpu.VMEM((8, TOK, UNITS), BF16),
            pltpu.VMEM((32, TOK, UNITS), BF16),
            pltpu.VMEM((32, TOK, UNITS), BF16),
            pltpu.VMEM((TOK, UNITS), F32),
            pltpu.VMEM((8, PAIR, FEAT), BF16),
            pltpu.VMEM((8, PAIR, FEAT), BF16),
            pltpu.VMEM((8, PAIR, FEAT), BF16),
            pltpu.VMEM((8, PAIR, FEAT), BF16),
            pltpu.VMEM((9, PAIR, FEAT), F32),
        ] + tree_sems * 3 + [dma((8,))] * 8 + [dma((5,))],
        compiler_params=pltpu.CompilerParams(
            collective_id=0, has_side_effects=True, vmem_limit_bytes=56 * 2**20),
        cost_estimate=pl.CostEstimate(flops=5_234_491_392, bytes_accessed=4_000_000, transcendentals=40_000),
    )(grad_out, gate_pre, up_pre, down_weight, gate_weight.T, up_weight.T)
    return pl.pallas_call(
        copy_out,
        out_shape=outs,
        in_specs=[vmem] * 2,
        out_specs=(vmem, vmem),
    )(input_grad, down_grad)


def solution(mesh):
    placed = (
        P("row", "col"),
        P("col", "row"),
        P("col", "row"),
        P("row", "col"),
        P("col", "row"),
        P("col", "row"),
    )
    return jax.shard_map(
        on_device,
        mesh=mesh,
        in_specs=placed,
        out_specs=(P("row", "col"), P("row", "col")),
        check_vma=False,
    )
```

time: 600 us -> 128 us (0.21)
  the two profiles are of different devices: /device:TPU:18 before, /device:TPU:33 now
where the time goes in v2:
time: 128 us; the launch traced here: 127 us
  Pallas kernels  127 us (99%)
    pallas_call x1, Pallas kernels, on_device(): pl.pallas_call(kernel, out_shape=outs, in_specs=[vmem] * 3 + [anywhere] *...  125 us

profile of v2, /device:TPU:33, one launch (start us, length us, event | category | flops | bytes accessed | tf_op | source)
XLA Modules:
  0.0 127.3 jit_solution(11676026616415094855)
XLA Ops:
  0.6 124.5 %shard_map.77 = (bf16[96,512]{1,0:T(8,128)(2,1)}, bf16[832,512]{1,0:T(8,128)(2,1)}) custom-call(bf16[96,512]{1,0:T(8,128)(2,1)} %grad_ref.1, bf16[48,832]{1,0:T(8,128)(2,1)} %gate_ref.1, bf16[48,832]{1,0:T(8,128)(2,1)} %up_ref.1, bf16[832,512]{1,0:T(8,128)(2,1)} %down_hbm.1, bf16[832,512]{1,0:T(8,128)(2,1)} %bitcast.2, bf16[832,512]{1,0:T(8,128)(2,1)} %bitcast.3), custom_call_target="tpu_custom_call" | custom-call | flops 5234491392 | bytes 4000000 | tf_op jit(solution)/shard_map/pallas_call | solution.py:500
  125.2 2.2 %shard_map.78 = (bf16[96,512]{1,0:T(8,128)(2,1)}, bf16[832,512]{1,0:T(8,128)(2,1)}) custom-call(bf16[96,512]{1,0:T(8,128)(2,1)} %get-tuple-element.4.a_ref, bf16[832,512]{1,0:T(8,128)(2,1)} %get-tuple-element.5.b_ref), custom_call_target="tpu_custom_call" | custom-call | tf_op jit(solution)/shard_map/pallas_call | solution.py:527

commit v3 on v2

--- a/solution.py
+++ b/solution.py
@@ -37,6 +37,7 @@
 LONG = NY // 2
 HOPS = (LONG, LONG - 1)
 DIRECT = (2, 1, -1)
+AFTER = {4: 3, 1: 4}
 COLUMNS = (0, 1, -1, 2)
 
 
@@ -386,6 +387,8 @@
         per_core(lambda which: scatter(which).open(off))
     for depth in (4, 3, 2, 1):
         per_core(lambda which: scatter(which).step(depth))
+        if depth in AFTER:
+            per_core(lambda which: hidden_gather(which).step(AFTER[depth]))
 
     def finish(which):
         hg[...] = scatter(which).result()
@@ -440,8 +443,17 @@
             block(-1)
     pass_on(1)
     pass_on(-1)
-    for time in (3, 4):
-        per_core(lambda which: hidden_gather(which).step(time))
+    def hidden_leaves(which):
+        for off in FAR_FIRST:
+            hidden_gather(which).leaves(off)
+
+    per_core(hidden_leaves)
+    all_rows = rows[...].reshape(NZ * 2 * PAIR, FEAT)
+    for start, size in ((0, 256), (256, 256), (512, 320)):
+        units = hid[:, :, :, pl.ds(start, size)].reshape(NY * NX * TOK, size)
+        down_grad_ref[pl.ds(start, size)] = lax.dot_general(
+            units, all_rows, (((0,), (0,)), ((), ())), preferred_element_type=F32).astype(BF16)
+
     for off in (2, -2):
         block(off)
     for off in (2, -2):
@@ -452,17 +464,6 @@
         pass_on(off)
     block(4)
     pass_on(4)
-
-    def hidden_leaves(which):
-        for off in FAR_FIRST:
-            hidden_gather(which).leaves(off)
-
-    per_core(hidden_leaves)
-    all_rows = rows[...].reshape(NZ * 2 * PAIR, FEAT)
-    for start, size in ((0, 256), (256, 256), (512, 320)):
-        units = hid[:, :, :, pl.ds(start, size)].reshape(NY * NX * TOK, size)
-        down_grad_ref[pl.ds(start, size)] = lax.dot_general(
-            units, all_rows, (((0,), (0,)), ((), ())), preferred_element_type=F32).astype(BF16)
 
     total = own[8]
     for off in range(1, NZ):

time: 128 us -> 124 us (0.969)
  Pallas kernels: 127 us -> 123 us
    pallas_call x1, Pallas kernels: 125 us -> 121 us  [on_device(): pl.pallas_call(kernel, out_shape=outs, in_specs=[vmem] * 3 + [anywhere] *...]
where the time goes in v3:
time: 124 us; the launch traced here: 123 us
  Pallas kernels  123 us (99%)
    pallas_call x1, Pallas kernels, on_device(): pl.pallas_call(kernel, out_shape=outs, in_specs=[vmem] * 3 + [anywhere] *...  121 us

profile of v3, /device:TPU:33, one launch (start us, length us, event | category | flops | bytes accessed | tf_op | source)
XLA Modules:
  0.0 123.5 jit_solution(5763689429254189321)
XLA Ops:
  0.6 120.6 %shard_map.77 = (bf16[96,512]{1,0:T(8,128)(2,1)}, bf16[832,512]{1,0:T(8,128)(2,1)}) custom-call(bf16[96,512]{1,0:T(8,128)(2,1)} %grad_ref.1, bf16[48,832]{1,0:T(8,128)(2,1)} %gate_ref.1, bf16[48,832]{1,0:T(8,128)(2,1)} %up_ref.1, bf16[832,512]{1,0:T(8,128)(2,1)} %down_hbm.1, bf16[832,512]{1,0:T(8,128)(2,1)} %bitcast.2, bf16[832,512]{1,0:T(8,128)(2,1)} %bitcast.3), custom_call_target="tpu_custom_call" | custom-call | flops 5234491392 | bytes 4000000 | tf_op jit(solution)/shard_map/pallas_call | solution.py:501
  121.3 2.2 %shard_map.78 = (bf16[96,512]{1,0:T(8,128)(2,1)}, bf16[832,512]{1,0:T(8,128)(2,1)}) custom-call(bf16[96,512]{1,0:T(8,128)(2,1)} %get-tuple-element.4.a_ref, bf16[832,512]{1,0:T(8,128)(2,1)} %get-tuple-element.5.b_ref), custom_call_target="tpu_custom_call" | custom-call | tf_op jit(solution)/shard_map/pallas_call | solution.py:528

commit v4 on v3

--- a/solution.py
+++ b/solution.py
@@ -435,14 +435,12 @@
 
     for time in (1, 2, 3, 4):
         per_core(lambda which: grads_gather(which).step(time))
-        if time == 2:
-            block(0)
-        if time == 3:
-            pass_on(0)
-            block(1)
-            block(-1)
-    pass_on(1)
-    pass_on(-1)
+        if time >= 2:
+            for off in y_offsets(time - 2):
+                pass_on(off)
+        if time <= 3:
+            for off in y_offsets(time - 1):
+                block(off)
     def hidden_leaves(which):
         for off in FAR_FIRST:
             hidden_gather(which).leaves(off)
@@ -454,10 +452,6 @@
         down_grad_ref[pl.ds(start, size)] = lax.dot_general(
             units, all_rows, (((0,), (0,)), ((), ())), preferred_element_type=F32).astype(BF16)
 
-    for off in (2, -2):
-        block(off)
-    for off in (2, -2):
-        pass_on(off)
     for off in (3, -3):
         block(off)
     for off in (3, -3):

time: 124 us -> 121 us (0.976)
  Pallas kernels: 123 us -> 120 us
    pallas_call x1, Pallas kernels: 121 us -> 117 us  [on_device(): pl.pallas_call(kernel, out_shape=outs, in_specs=[vmem] * 3 + [anywhere] *...]
where the time goes in v4:
time: 121 us; the launch traced here: 120 us
  Pallas kernels  120 us (99%)
    pallas_call x1, Pallas kernels, on_device(): pl.pallas_call(kernel, out_shape=outs, in_specs=[vmem] * 3 + [anywhere] *...  117 us

profile of v4, /device:TPU:33, one launch (start us, length us, event | category | flops | bytes accessed | tf_op | source)
XLA Modules:
  0.0 120.2 jit_solution(2994697329387833450)
XLA Ops:
  0.6 117.4 %shard_map.77 = (bf16[96,512]{1,0:T(8,128)(2,1)}, bf16[832,512]{1,0:T(8,128)(2,1)}) custom-call(bf16[96,512]{1,0:T(8,128)(2,1)} %grad_ref.1, bf16[48,832]{1,0:T(8,128)(2,1)} %gate_ref.1, bf16[48,832]{1,0:T(8,128)(2,1)} %up_ref.1, bf16[832,512]{1,0:T(8,128)(2,1)} %down_hbm.1, bf16[832,512]{1,0:T(8,128)(2,1)} %bitcast.2, bf16[832,512]{1,0:T(8,128)(2,1)} %bitcast.3), custom_call_target="tpu_custom_call" | custom-call | flops 5234491392 | bytes 4000000 | tf_op jit(solution)/shard_map/pallas_call | solution.py:495
  118.0 2.2 %shard_map.78 = (bf16[96,512]{1,0:T(8,128)(2,1)}, bf16[832,512]{1,0:T(8,128)(2,1)}) custom-call(bf16[96,512]{1,0:T(8,128)(2,1)} %get-tuple-element.4.a_ref, bf16[832,512]{1,0:T(8,128)(2,1)} %get-tuple-element.5.b_ref), custom_call_target="tpu_custom_call" | custom-call | tf_op jit(solution)/shard_map/pallas_call | solution.py:522
